TPU v7x, 256 devices: a whole 4x4x8 slice. The times are simulated.
256 devices in a mesh: dp: 4 (over x), ctx: 64 (over z, y, core).
Axes of the slice: x: 4, y: 4, z: 8, core: 2. Of those that a mesh axis runs over, the one named last changes fastest.
Arguments:
- saved_pre: bfloat16 [32768, 8, 1024], P(('dp', 'ctx')), may hold values from -6 to 6
- layer_grad: bfloat16 [32768, 2304], P(('dp', 'ctx')), may hold values from -4 to 4
- router_weight: bfloat16 [32768, 8], P(('dp', 'ctx')), may hold values from 0.049804688 to 0.5
- routes: int32 [32768, 8], P(('dp', 'ctx')), may hold values from 0 to 127, all different within a row; in each aligned block of 128 rows (0 to 127, 128 to 255, ...) at most 9 rows name the same one
- queries: bfloat16 [4, 8192, 1024], P('dp', 'ctx'), may hold values from -0.625 to 0.625
- key_vectors: bfloat16 [4, 8192, 1024], P('dp', 'ctx'), may hold values from -2 to 2
- value_vectors: bfloat16 [4, 8192, 1024], P('dp', 'ctx'), may hold values from -2 to 2
- head_grad: bfloat16 [4, 8192, 1024], P('dp', 'ctx'), may hold values from -6 to 6
- log_gate: float32 [4, 8192, 1024], P('dp', 'ctx'), may hold values from -1 to 0
Outputs:
- key_grad: bfloat16 [4, 8192, 1024], P('dp', 'ctx')
- value_grad: bfloat16 [4, 8192, 1024], P('dp', 'ctx')
- down_grad: bfloat16 [128, 512, 2304], P('ctx', None, 'dp')
Inputs may be any that keep to these rules, and one draw needn't show every extreme that they name: `routes`: within the rows of one device each expert is named by at most 9 rows, a bound that some block reaches; each row names 8 different experts.
All inputs are finite; a program needn't handle non-finite values.
Results may differ from a plain program's by a relative error of at most 0.0057.
Values may be sent and summed in bfloat16 or wider, within the bound.
A program may use at most 192 MiB of HBM per device.

v0:
```python
import jax
import jax.numpy as jnp
from jax import lax
from jax.sharding import PartitionSpec as P

FF = 512
HEADS = 16
HEAD_K = 64
TOP = 8
EXP_DEV = 2


def carried_in(array, axis, combine, identity):
    peers, mine = (lax.axis_size(axis), lax.axis_index(axis))
    everything = jax.tree.map(lambda part: lax.all_gather(part, axis), array)
    start = jax.tree.map(
        lambda part, zero: jnp.broadcast_to(jnp.asarray(zero, part.dtype), part.shape),
        array,
        identity,
    )

    def hop(k, before):
        at = peers - 1 - k
        reached = at > mine
        new = combine(before, jax.tree.map(lambda part: part[at], everything))
        return jax.tree.map(lambda a, b: jnp.where(reached, a, b), new, before)

    return lax.fori_loop(0, peers, hop, start)


def join_later(earlier, later):
    return (later[0] * earlier[0], later[0][:, :, None] * earlier[1] + later[1])


def head_backward(queries, key_vectors, value_vectors, head_grad, log_gate):
    steps = queries.shape[1]
    shape = (steps, HEADS, HEAD_K)
    upper_limit = lax.Precision.HIGH
    query_b = queries[0].reshape(shape)
    key_b = key_vectors[0].reshape(shape)
    value_b = value_vectors[0].reshape(shape)
    grad_b = head_grad[0].reshape(shape)
    gradient_float = grad_b.astype(jnp.float32)
    value_float = value_b.astype(jnp.float32)
    cumulative = jnp.cumsum(log_gate[0].reshape(shape), axis=0)
    last = cumulative[-1]
    scaled_query = query_b.astype(jnp.float32) * jnp.exp(cumulative)
    key_scaled = key_b.astype(jnp.float32) * jnp.exp(-cumulative)
    tail = jnp.exp(last[None] - cumulative)
    block_sum = jnp.einsum(
        "moe,mob->oeb",
        scaled_query,
        gradient_float,
        precision=upper_limit,
        preferred_element_type=jnp.float32,
    )
    identity = (
        jnp.ones((HEADS, HEAD_K), jnp.float32),
        jnp.zeros((HEADS, HEAD_K, HEAD_K), jnp.float32),
    )
    _, carried_state = carried_in((jnp.exp(last), block_sum), "ctx", join_later, identity)
    order = jnp.arange(steps)
    upper = (order[:, None] <= order[None, :]).astype(jnp.float32)
    value_dot = (
        jnp.einsum("thv,uhv->htu", value_b, grad_b, preferred_element_type=jnp.float32) * upper
    )
    key_out = jnp.exp(-cumulative) * jnp.einsum(
        "htu,uhk->thk",
        value_dot,
        scaled_query,
        precision=upper_limit,
        preferred_element_type=jnp.float32,
    )
    key_out = key_out + tail * jnp.einsum(
        "pbz,bcz->pbc",
        value_float,
        carried_state,
        precision=upper_limit,
        preferred_element_type=jnp.float32,
    )
    key_dot = (
        jnp.einsum(
            "thk,uhk->htu",
            key_scaled,
            scaled_query,
            precision=upper_limit,
            preferred_element_type=jnp.float32,
        )
        * upper
    )
    value_out = jnp.einsum(
        "htu,uhv->thv",
        key_dot,
        gradient_float,
        precision=upper_limit,
        preferred_element_type=jnp.float32,
    )
    value_out = value_out + jnp.einsum(
        "eqj,qjp->eqp",
        key_b.astype(jnp.float32) * tail,
        carried_state,
        precision=upper_limit,
        preferred_element_type=jnp.float32,
    )
    width = HEADS * HEAD_K
    return (
        key_out.reshape(1, steps, width).astype(jnp.bfloat16),
        value_out.reshape(1, steps, width).astype(jnp.bfloat16),
    )


def on_device(
    saved_pre,
    layer_grad,
    router_weight,
    routes,
    queries,
    key_vectors,
    value_vectors,
    head_grad,
    log_gate,
):
    key_grad, value_grad = head_backward(queries, key_vectors, value_vectors, head_grad, log_gate)
    rows = layer_grad.shape[0]
    features = layer_grad.shape[1]
    hidden_pair = saved_pre.shape[2]
    ctx_count = lax.axis_size("ctx")
    experts = EXP_DEV * ctx_count
    capacity = rows * TOP * 9 // (8 * experts)
    pairs = rows * TOP
    flat_ids = routes.reshape(-1)
    onehot = (flat_ids[:, None] == jnp.arange(experts, dtype=jnp.int32)[None, :]).astype(jnp.int32)
    ranking = jnp.sum((jnp.cumsum(onehot, axis=0) - 1) * onehot, axis=1)
    target = flat_ids * capacity + ranking
    pair_index = jnp.arange(pairs, dtype=jnp.int32)
    source = pair_index // TOP
    table = jnp.full((experts * capacity,), rows, jnp.int32).at[target].set(source)
    pair_table = jnp.full((experts * capacity,), pairs, jnp.int32).at[target].set(pair_index)
    slot_weight = (
        jnp.zeros((experts * capacity,), jnp.float32)
        .at[target]
        .set(router_weight.reshape(-1).astype(jnp.float32))
    )
    flat_pre = jnp.concatenate(
        [saved_pre.reshape(pairs, hidden_pair), jnp.zeros((1, hidden_pair), saved_pre.dtype)]
    )
    padded_grad = jnp.concatenate([layer_grad, jnp.zeros((1, features), layer_grad.dtype)])
    sent_pre = flat_pre[pair_table]
    sent_grad = (padded_grad[table].astype(jnp.float32) * slot_weight[:, None]).astype(jnp.bfloat16)
    got_pre, got_grad = (
        lax.all_to_all(sent_pre, "ctx", split_axis=0, concat_axis=0, tiled=True),
        lax.all_to_all(sent_grad, "ctx", split_axis=0, concat_axis=0, tiled=True),
    )
    got_pre = got_pre.reshape(ctx_count, EXP_DEV, capacity, hidden_pair).astype(jnp.float32)
    got_grad = got_grad.reshape(ctx_count, EXP_DEV, capacity, features)
    pair_hidden = (jax.nn.silu(got_pre[..., :FF]) * got_pre[..., FF:]).astype(jnp.bfloat16)
    partial_grad = jnp.einsum(
        "secf,secd->efd", pair_hidden, got_grad, preferred_element_type=jnp.float32
    )
    down_grad = lax.psum_scatter(partial_grad, "dp", scatter_dimension=2, tiled=True).astype(
        jnp.bfloat16
    )
    return (key_grad, value_grad, down_grad)


def solution(mesh):
    return jax.shard_map(
        on_device,
        mesh=mesh,
        in_specs=(
            P(("dp", "ctx"), None, None),
            P(("dp", "ctx"), None),
            P(("dp", "ctx"), None),
            P(("dp", "ctx"), None),
            P("dp", "ctx", None),
            P("dp", "ctx", None),
            P("dp", "ctx", None),
            P("dp", "ctx", None),
            P("dp", "ctx", None),
        ),
        out_specs=(P("dp", "ctx", None), P("dp", "ctx", None), P("ctx", None, "dp")),
        check_vma=False,
    )
```

profile of v0, /device:TPU:1, one launch (start us, length us, event | category | flops | bytes accessed | tf_op | source)
XLA Modules:
  0.0 605.4 jit_solution(3844378252951669418)
XLA Ops:
  10.8 4.3 scatter_custom_fusion
  15.1 1.8 concatenate.6
  16.9 5.0 gather_fusion
  21.9 4.3 all_to_all.10
  26.2 13.5 %all-to-all-start = ((bf16[64,18,1024]{2,1,0:T(8,128)(2,1)}), bf16[64,18,1024]{2,1,0:T(8,128)(2,1)}, u32[]{:S(2)}, u32[]{:S(2)}) async-start(bf16[64,18,1024]{2,1,0:T(8,128)(2,1)} %all_to_all.10), calls=%async_computation | async-start | bytes 6291456 | tf_op jit(solution)/shard_map/all_to_all | solution.py:151
  39.7 4.3 scatter_custom_fusion.1
  44.1 6.2 %gather_fusion.1 = bf16[1152,2304]{1,0:T(8,128)(2,1)} fusion(bf16[129,2304]{1,0:T(8,128)(2,1)S(1)} %concatenate.7, s32[2048]{0:T(1024)S(1)} %pad_clamp_fusion), kind=kCustom, calls=%fused_computation.1 | custom fusion | bytes 10621440 | tf_op jit(solution)/shard_map/gather | solution.py:149
  50.3 9.0 %reshape.133 = f32[64,18,2304]{2,1,0:T(8,128)} reshape(bf16[1152,2304]{1,0:T(8,128)(2,1)} %gather_fusion.1) | data formatting | bytes 15925248 | tf_op jit(solution)/shard_map/convert_element_type | solution.py:149
  59.5 4.3 scatter_custom_fusion.2
  64.0 8.6 %multiply_convert_fusion = bf16[64,18,2304]{2,1,0:T(8,128)(2,1)} fusion(f32[64,18,2304]{2,1,0:T(8,128)} %reshape.133, f32[64,18]{1,0:T(8,128)S(1)} %mul.115), kind=kLoop, calls=%fused_computation.8 | loop fusion | flops 5308416 | bytes 15929856 | tf_op jit(solution)/shard_map/convert_element_type | solution.py:149
  72.6 39.5 %all-to-all-done = bf16[64,18,1024]{2,1,0:T(8,128)(2,1)} async-done(((bf16[64,18,1024]{2,1,0:T(8,128)(2,1)}), bf16[64,18,1024]{2,1,0:T(8,128)(2,1)}, u32[]{:S(2)}, u32[]{:S(2)}) %all-to-all-start) | async-done | bytes 2359328 | tf_op jit(solution)/shard_map/all_to_all | solution.py:151
  112.1 6.8 %all-to-all-start.1 = ((bf16[64,18,2304]{2,1,0:T(8,128)(2,1)}), bf16[64,18,2304]{2,1,0:T(8,128)(2,1)}, u32[]{:S(2)}, u32[]{:S(2)}) async-start(bf16[64,18,2304]{2,1,0:T(8,128)(2,1)} %multiply_convert_fusion), calls=%async_computation.1 | async-start | bytes 14155776 | tf_op jit(solution)/shard_map/all_to_all | solution.py:152
  119.2 3.2 copy.135
  122.4 2.8 convert.5
  125.2 148.8 %all-to-all-done.1 = bf16[64,18,2304]{2,1,0:T(8,128)(2,1)} async-done(((bf16[64,18,2304]{2,1,0:T(8,128)(2,1)}), bf16[64,18,2304]{2,1,0:T(8,128)(2,1)}, u32[]{:S(2)}, u32[]{:S(2)}) %all-to-all-start.1) | async-done | bytes 5308448 | tf_op jit(solution)/shard_map/all_to_all | solution.py:152
  273.9 4.3 copy.137
  278.3 6.5 %convolution_bitcast_fusion = f32[2,512,2304]{1,2,0:T(8,128)} fusion(bf16[64,2,9,2304]{3,0,2,1:T(8,128)(2,1)S(1)} %bitcast.73, f32[64,2,9,1024]{3,0,2,1:T(8,128)S(1)} %copy-done), kind=kOutput, calls=%fused_computation.9 | convolution fusion | flops 2721447936 | bytes 19464192 | tf_op jit(solution)/shard_map/secf,secd->efd/dot_general | solution.py:157
  287.2 23.3 %fusion.28 = f32[128,16,64]{2,1,0:T(8,128)S(1)} fusion(f32[128,16,64]{2,1,0:T(8,128)S(1)} %copy.118), kind=kOutput, calls=%fused_computation.64 | output fusion | flops 16646144 | bytes 1048576 | tf_op jit(solution)/shard_map/jit(cumsum)/reduce_window_sum | solution.py:45
  311.6 1.6 copy.124
  316.2 1.8 copy.122
  318.0 56.9 %all_gather.10 = f32[64,16,64]{2,1,0:T(8,128)} all-gather(f32[1,16,64]{2,1,0:T(8,128)S(1)} %get-tuple-element.183), channel_id=1, replica_groups=mesh['dp'=4,'ctx'=64] {'ctx'}, dimensions={0}, use_global_device_ids=true | all-gather | bytes 266240 | tf_op jit(solution)/shard_map/all_gather | solution.py:15
  376.2 2.0 convolution_multiply_fusion
  378.2 2.9 convert_element_type.104
  381.1 76.1 %all-gather.3.cloned.1.call-done = f32[1024,64,64]{2,1,0:T(8,128)} async-done(((f32[16,64,64]{2,1,0:T(8,128)}), f32[1024,64,64]{2,1,0:T(8,128)}) %all-gather.3.cloned.1.call-update) | async-done | bytes 16777232 | tf_op jit(solution)/shard_map/all_gather | solution.py:15
  457.2 135.0 %while.16 = (s32[]{:T(128)}, f32[16,64,64]{2,1,0:T(8,128)S(1)}, s32[]{:T(128)}, f32[64,16,64]{2,1,0:T(8,128)}, f32[64,16,64,64]{3,2,1,0:T(8,128)}, /*index=5*/s32[]{:T(128)}, s32[]{:T(128)}, s32[]{:T(128)}, s32[]{:T(128)}) while((s32[]{:T(128)}, f32[16,64,64]{2,1,0:T(8,128)S(1)}, s32[]{:T(128)}, f32[64,16,64]{2,1,0:T(8,128)}, ...), condition=%wide.region_2.3_spmd.clone, body=%wide.region_1.2_spmd.clone.sunk | while | flops 262152 | bytes 798887 | solution.py:28
  457.9 1.4 fusion.45
  460.0 1.4 fusion.45
  462.1 1.4 fusion.45
  464.2 1.4 fusion.45
  466.3 1.4 fusion.45
  468.4 1.4 fusion.45
  470.6 1.4 fusion.45
  472.7 1.4 fusion.45
  474.8 1.4 fusion.45
  476.9 1.4 fusion.45
  479.0 1.4 fusion.45
  481.1 1.4 fusion.45
  483.2 1.4 fusion.45
  485.3 1.4 fusion.45
  487.4 1.4 fusion.45
  489.6 1.4 fusion.45
  491.7 1.4 fusion.45
  493.8 1.4 fusion.45
  495.9 1.4 fusion.45
  498.0 1.4 fusion.45
  504.3 1.4 fusion.45
  506.4 1.4 fusion.45
  510.7 1.4 fusion.45
  512.8 1.4 fusion.45
  519.1 1.4 fusion.45
  525.4 1.4 fusion.45
  531.8 1.4 fusion.45
  538.1 1.4 fusion.45
  544.4 1.4 fusion.45
  546.5 1.4 fusion.45
  550.8 1.4 fusion.45
  552.9 1.4 fusion.45
  559.2 1.4 fusion.45
  565.5 1.4 fusion.45
  571.9 1.4 fusion.45
  578.2 1.4 fusion.45
  584.5 1.4 fusion.45
  586.6 1.4 fusion.45
  590.9 1.4 fusion.45
  (152 shorter events, 96.2 us)
Async XLA Ops:
  26.2 13.5 %copy-start.2 = (bf16[128,2304]{1,0:T(8,128)(2,1)S(1)}, bf16[128,2304]{1,0:T(8,128)(2,1)}, u32[]{:S(2)}) copy-start(bf16[128,2304]{1,0:T(8,128)(2,1)} %param.12) | copy-start | bytes 1769476
  26.2 86.0 %all-to-all-start = ((bf16[64,18,1024]{2,1,0:T(8,128)(2,1)}), bf16[64,18,1024]{2,1,0:T(8,128)(2,1)}, u32[]{:S(2)}, u32[]{:S(2)}) async-start(bf16[64,18,1024]{2,1,0:T(8,128)(2,1)} %all_to_all.10), calls=%async_computation | async-start | bytes 6291456 | tf_op jit(solution)/shard_map/all_to_all | solution.py:151
  50.3 9.0 %copy-start.6 = (bf16[128,8]{0,1:T(8,128)(2,1)S(1)}, bf16[128,8]{0,1:T(8,128)(2,1)}, u32[]{:S(2)}) copy-start(bf16[128,8]{0,1:T(8,128)(2,1)} %param.13) | copy-start | bytes 6148
  112.1 161.8 %all-to-all-start.1 = ((bf16[64,18,2304]{2,1,0:T(8,128)(2,1)}), bf16[64,18,2304]{2,1,0:T(8,128)(2,1)}, u32[]{:S(2)}, u32[]{:S(2)}) async-start(bf16[64,18,2304]{2,1,0:T(8,128)(2,1)} %multiply_convert_fusion), calls=%async_computation.1 | async-start | bytes 14155776 | tf_op jit(solution)/shard_map/all_to_all | solution.py:152
  119.0 259.2 %reduce-scatter.2.cloned.1.call-start = ((), (), s32[]{:S(2)}) async-start(), calls=%async_computation.3 | async-start | bytes 11796480 | tf_op jit(solution)/shard_map/reduce_scatter | solution.py:160
  273.9 4.4 copy-start
  284.8 1.0 copy-start.3
  284.8 1.7 copy-start.4
  284.8 172.4 %all-gather.3.cloned.1.call-start = ((), (), s32[]{:S(2)}) async-start(), calls=%async_computation.4 | async-start | bytes 34078720 | tf_op jit(solution)/shard_map/all_gather | solution.py:15
  310.5 2.7 copy-start.5
  592.3 2.0 copy-start.1
Sparse Core Ops, SparseCore 0:
  284.9 91.4 reduce-scatter.1
Sparse Core Ops, SparseCore 1:
  314.7 142.4 all-gather.2
where the time goes:
time: 612 us; the launch traced here: 605 us
  waiting for transfers between devices  264 us (43%)
  other arithmetic  128 us (21%)
  local copies, waits for them, and re-layouts  103 us (17%)
  blocking collectives  56.9 us (9%)
  starting transfers between devices  20.6 us (3%)
  between operations  15.8 us (3%)
  matrix products  15 us (2%)
    all_to_all x1, waiting for transfers between devices, on_device(): lax.all_to_all(sent_grad, 'ctx', split_axis=0, concat_axis=0, tiled=True)  149 us
    select_n x64, other arithmetic, hop(): return jax.tree.map(lambda a, b: jnp.where(reached, a, b), new, before)  88.2 us
    all_gather x1, waiting for transfers between devices, carried_in(): everything = jax.tree.map(lambda part: lax.all_gather(part, axis), array)  76.1 us
    all_gather x1, blocking collectives, carried_in(): everything = jax.tree.map(lambda part: lax.all_gather(part, axis), array)  56.9 us
    mul x64, local copies, waits for them, and re-layouts, join_later(): return (later[0] * earlier[0], later[0][:, :, None] * earlier[1] + later[1])  45 us
    all_to_all x1, waiting for transfers between devices, on_device(): lax.all_to_all(sent_pre, 'ctx', split_axis=0, concat_axis=0, tiled=True)  39.5 us
    another operation x1, other arithmetic, head_backward(): cumulative = jnp.cumsum(log_gate[0].reshape(shape), axis=0)  23.3 us
    all_to_all x1, starting transfers between devices, on_device(): lax.all_to_all(sent_pre, 'ctx', split_axis=0, concat_axis=0, tiled=True)  13.5 us
  transfers between devices with their start and end apart: 4, of which 3 were waited for; matrix products, arithmetic and copies ran while one was open for 13% of the time, Pallas kernels for 0%

commit v1 on v0

v1 whole, which is shorter than its diff:
```python
import functools

import jax
import jax.numpy as jnp
from jax import lax
from jax.experimental import pallas as pl
from jax.experimental.pallas import tpu as pltpu
from jax.sharding import PartitionSpec as P

FF = 512
TOK = 128
D = 2304
Z = 8
W = 8
DP = 4
CAP = 9
TOP = 8
PAIRS = TOK * TOP
PIECES = 6
PC = D // PIECES
UNIT = D // 12
OWN = D // DP
LANES = 128
MESH = pl.DeviceIdType.MESH
F32 = jnp.float32
BF16 = jnp.bfloat16


def iota(shape, dim):
    return lax.broadcasted_iota(jnp.int32, shape, dim)


def dot(a, b):
    return lax.dot_general(a, b, (((1,), (0,)), ((), ())), preferred_element_type=F32)


def dot_nt(a, b):
    return lax.dot_general(a, b, (((1,), (1,)), ((), ())), preferred_element_type=F32)


def dot_tn(a, b):
    return lax.dot_general(a, b, (((0,), (0,)), ((), ())), preferred_element_type=F32)


def split2(x):
    hi = x.astype(BF16)
    return hi, (x - hi.astype(F32)).astype(BF16)


def kernel(
    pre_ref, g_ref, rt_ref, wt_ref, q_ref, k_ref, v_ref, do_ref, lg_ref,
    kg_ref, vg_ref, dg_ref,
    ga, hid, sh, hin, pa, hy, hr, hm, yb, rx, xt, su, rs, acc,
    cum, a_s, a_r, b_s, b_r, cl, c_s, c_r,
    ag_ss, ag_rs, hz_ss, hz_rs, hw_ss, hw_rs, y_ss, y_rs, rs_ss, rs_rs,
    a_ss, a_rs, b_ss, b_rs, c_ss, c_rs,
):
    dp = lax.axis_index("dp")
    ctx = lax.axis_index("ctx")
    z = ctx // W
    w = ctx % W

    def z_peer(t):
        return {"ctx": t * W + w}

    def w_peer(t):
        return {"ctx": z * W + t}

    def remote(src, dst, ss, rsem, dev):
        return pltpu.make_async_remote_copy(
            src_ref=src, dst_ref=dst, send_sem=ss, recv_sem=rsem, device_id=dev, device_id_type=MESH
        )

    barrier = pltpu.get_barrier_semaphore()
    for o in range(1, Z):
        pl.semaphore_signal(barrier, inc=1, device_id=z_peer((z + o) % Z), device_id_type=MESH)
        pl.semaphore_signal(barrier, inc=1, device_id=w_peer((w + o) % W), device_id_type=MESH)
    for o in range(1, DP):
        pl.semaphore_signal(barrier, inc=1, device_id={"dp": (dp + o) % DP}, device_id_type=MESH)
    pl.semaphore_wait(barrier, (Z - 1) + (W - 1) + (DP - 1))

    first_piece = (2 + (3 * dp) // 2) % PIECES

    def piece_of(i):
        return (first_piece + i) % PIECES

    def hops(i, way):
        return 4 if (i % 2 == 0) == (way == 0) else 3

    def ag_copy(i, way, step):
        src = (z - step + Z) % Z if way == 0 else (z + step) % Z
        to = (z + 1) % Z if way == 0 else (z + Z - 1) % Z
        return remote(ga.at[i, src], ga.at[i, src], ag_ss.at[i, way, step], ag_rs.at[i, way, step], z_peer(to))

    def ag_arrival(i, way, step):
        src = (z - 1 - step + 2 * Z) % Z if way == 0 else (z + 1 + step) % Z
        return remote(
            ga.at[i, src], ga.at[i, src], ag_ss.at[i, way, step], ag_rs.at[i, way, step], z_peer((z + 1) % Z)
        )

    for i in range(PIECES):
        ga[i, z] = g_ref[:, pl.ds(pl.multiple_of(piece_of(i) * PC, LANES), PC)]
        ag_copy(i, 0, 0).start()
        ag_copy(i, 1, 0).start()

    def forward(i, step):
        for way in range(2):
            if step < hops(i, way):
                ag_arrival(i, way, step - 1).wait_recv()
                ag_copy(i, way, step).start()

    def hidden_block(n, carry):
        x = pre_ref[pl.ds(n * 16, 16)].astype(F32).reshape(LANES, 2 * FF)
        gate, up = x[:, :FF], x[:, FF:]
        hid[pl.ds(pl.multiple_of(n * LANES, LANES), LANES), :] = (gate / (1.0 + jnp.exp(-gate)) * up).astype(BF16)
        return carry

    lax.fori_loop(0, PAIRS // LANES, hidden_block, 0)

    named = iota((LANES, PAIRS), 0) == rt_ref[...]
    named_f = jnp.where(named, 1.0, 0.0)
    token_of = jnp.where(iota((PAIRS, TOK), 0) // TOP == iota((PAIRS, TOK), 1), 1.0, 0.0).astype(BF16)
    by_token = dot(named_f.astype(BF16), token_of)
    weight = dot(jnp.where(named, wt_ref[...], 0.0).astype(BF16), token_of)
    before = jnp.where(iota((TOK, TOK), 0) < iota((TOK, TOK), 1), 1.0, 0.0).astype(BF16)
    rank = dot(by_token.astype(BF16), before)
    rank_pair = dot_nt(rank.astype(BF16), token_of)
    rank_pair = jnp.where(named, rank_pair, -1.0)
    rank = jnp.where(by_token > 0.5, rank, -1.0)
    for r in range(CAP):
        pa[r] = jnp.where(rank_pair == float(r), 1.0, 0.0).astype(BF16)
        sh[r, :, FF:] = jnp.where(rank == float(r), weight, 0.0).astype(BF16)

    def sort_block(n, carry):
        pick = pa[pl.ds(3 * n, 3)].reshape(3 * LANES, PAIRS)
        sh[pl.ds(3 * n, 3), :, :FF] = dot(pick, hid[...]).astype(BF16).reshape(3, LANES, FF)
        return carry

    lax.fori_loop(0, 3, sort_block, 0)

    def hz_copy(t):
        return remote(sh.at[:, pl.ds(pl.multiple_of(16 * t, 16), 16)], hin.at[:, z], hz_ss.at[t], hz_rs.at[z], z_peer(t))

    def hz_arrival(s):
        return remote(hin.at[:, z], hin.at[:, s], hz_ss.at[s], hz_rs.at[s], z_peer(s))

    for o in (4, 3, 5, 2, 6, 1, 7):
        hz_copy((z + o) % Z).start()
    hin[:, z] = sh[:, pl.ds(pl.multiple_of(16 * z, 16), 16)]

    lane = iota((LANES, LANES), 1)
    low = lane < 64
    low64 = iota((64, LANES), 1) < 64
    tri = jnp.where(iota((TOK, TOK), 1) <= iota((TOK, TOK), 0), 1.0, 0.0).astype(BF16)

    def attend_first(j, carry):
        at = pl.ds(pl.multiple_of(j * LANES, LANES), LANES)
        x = lg_ref[:, at]
        hi, rest = split2(x)
        mid, lo = split2(x - hi.astype(F32))
        total = dot(tri, hi) + (dot(tri, mid) + dot(tri, lo))
        cum[:, at] = total
        qh, ql = split2(q_ref[:, at].astype(F32) * jnp.exp(total))
        do = do_ref[:, at]
        s = dot_tn(qh, do) + dot_tn(ql, do)
        last = jnp.broadcast_to(total.T[:, TOK - 1 :], (LANES, LANES))
        a_s[j, :64] = jnp.where(low64, s[:64], s[64:])
        a_s[j, 64:] = jnp.where(low64, last[:64], last[64:])
        return carry

    lax.fori_loop(0, W, attend_first, 0)

    def a_copy(t):
        return remote(a_s.at[t], a_r.at[w], a_ss.at[t], a_rs.at[w], w_peer(t))

    def a_arrival(s):
        return remote(a_s.at[s], a_r.at[s], a_ss.at[s], a_rs.at[s], w_peer(s))

    for o in range(1, W):
        a_copy((w + o) % W).start()
    a_r[w] = a_s[w]

    def b_copy(t):
        return remote(b_s, b_r.at[z], b_ss.at[t], b_rs.at[z], z_peer(t))

    def b_arrival(s):
        return remote(b_s, b_r.at[s], b_ss.at[s], b_rs.at[s], z_peer(s))

    def attend_plane():
        for o in range(1, W):
            a_arrival((w + o) % W).wait_recv()
        c = jnp.zeros((64, LANES), F32)
        d = jnp.zeros((64, LANES), F32)
        for b in range(W - 1, -1, -1):
            cl[b, :64] = c
            cl[b, 64:] = d
            ld = a_r[b, 64:]
            c = a_r[b, :64] + jnp.exp(ld) * c
            d = d + ld
        b_s[:64] = c
        b_s[64:] = d
        for t in range(Z - 1):
            @pl.when(t < z)
            def _():
                b_copy(t).start()

    def c_copy(t):
        return remote(c_s.at[t], c_r.at[w], c_ss.at[t], c_rs.at[w], w_peer(t))

    def c_arrival(s):
        return remote(c_s.at[s], c_r.at[s], c_ss.at[s], c_rs.at[s], w_peer(s))

    def attend_carry():
        acc[:64, :LANES] = jnp.zeros((64, LANES), F32)
        for s in range(Z - 1, 0, -1):
            @pl.when(s > z)
            def _():
                b_arrival(s).wait_recv()
                acc[:64, :LANES] = b_r[s, :64] + jnp.exp(b_r[s, 64:]) * acc[:64, :LANES]
        x = acc[:64, :LANES]
        for b in range(W):
            c_s[b] = cl[b, :64] + jnp.exp(cl[b, 64:]) * x
        for o in range(1, W):
            c_copy((w + o) % W).start()
        c_r[w] = c_s[w]

    def attend_last():
        for o in range(1, W):
            c_arrival((w + o) % W).wait_recv()
        later = iota((TOK, TOK), 0) <= iota((TOK, TOK), 1)

        def pair(j, carry):
            at = pl.ds(pl.multiple_of(j * LANES, LANES), LANES)
            total = cum[:, at]
            middle = total[63:64]
            ek = jnp.exp(middle - total)
            tail = jnp.exp(total[TOK - 1 :] - total)
            k = k_ref[:, at].astype(F32)
            v = v_ref[:, at]
            do = do_ref[:, at]
            qs = q_ref[:, at].astype(F32) * jnp.exp(total - middle)
            ks = k * ek
            qh, ql = split2(qs)
            vo = jnp.zeros((TOK, LANES), F32)
            ko = jnp.zeros((TOK, LANES), F32)
            for half in (low, jnp.logical_not(low)):
                kh, kl = split2(jnp.where(half, ks, 0.0))
                scores = dot_nt(kh, qh) + (dot_nt(kh, ql) + dot_nt(kl, qh))
                sh_, sl_ = split2(jnp.where(later, scores, 0.0))
                dom = jnp.where(half, do.astype(F32), 0.0).astype(BF16)
                vo = vo + (dot(sh_, dom) + dot(sl_, dom))
                vm = jnp.where(half, v.astype(F32), 0.0).astype(BF16)
                bh, bl = split2(jnp.where(later, dot_nt(vm, do), 0.0))
                qmh, qml = split2(jnp.where(half, qs, 0.0))
                ko = ko + (dot(bh, qmh) + (dot(bl, qmh) + dot(bh, qml)))
            c = c_r[j]
            ch, clo = split2(jnp.concatenate([jnp.where(low64, c, 0.0), jnp.where(low64, 0.0, c)], axis=0))
            th, tl = split2(k * tail)
            vo = vo + (dot(th, ch) + (dot(th, clo) + dot(tl, ch)))
            ko = ek * ko + tail * (dot_nt(v, ch) + dot_nt(v, clo))
            kg_ref[:, at] = ko.astype(BF16)
            vg_ref[:, at] = vo.astype(BF16)
            return carry

        lax.fori_loop(0, W, pair, 0)

    def hw_copy(t):
        return remote(
            hy.at[:, pl.ds(pl.multiple_of(16 * t, 16), 16)], hr.at[pl.ds(CAP * w, CAP)], hw_ss.at[t], hw_rs.at[w], w_peer(t)
        )

    def hw_arrival(s):
        return remote(hr.at[pl.ds(CAP * s, CAP)], hr.at[pl.ds(CAP * s, CAP)], hw_ss.at[s], hw_rs.at[s], w_peer(s))

    def hidden_plane():
        for o in range(1, Z):
            hz_arrival((z + o) % Z).wait_recv()
        row = iota((LANES, LANES), 0)
        col = iota((LANES, LANES), 1)
        same = (row // 2) % 8 == col // 16
        place = jnp.where(same & (col % 16 == 2 * (row // 16) + row % 2), 1.0, 0.0).astype(BF16)
        source = (row // 2) % 8

        def one(r, carry):
            x = dot(place, hin[r].reshape(LANES, FF + LANES))
            hy[r] = x[:, :FF].astype(BF16)
            p = x[:, FF:]
            for s in range(Z):
                pa[r, :, s * LANES : (s + 1) * LANES] = jnp.where(source == s, p, 0.0).astype(BF16)
            return carry

        lax.fori_loop(0, CAP, one, 0)
        for o in range(1, W):
            hw_copy((w + o) % W).start()
        hr[pl.ds(CAP * w, CAP)] = hy[:, pl.ds(pl.multiple_of(16 * w, 16), 16)]

    def hidden_wide():
        for o in range(1, W):
            hw_arrival((w + o) % W).wait_recv()

        def one(m, carry):
            x = hr[pl.ds(8 * m, 8)].reshape(LANES, FF).astype(F32)
            first = iota((LANES, FF), 0) % 2 == 0
            at = pl.ds(pl.multiple_of(m * LANES, LANES), LANES)
            hm[at, :FF] = jnp.where(first, x, 0.0).astype(BF16)
            hm[at, FF:] = jnp.where(first, 0.0, x).astype(BF16)
            return carry

        lax.fori_loop(0, CAP, one, 0)

    def y_copy(i, t):
        return remote(
            yb.at[i, :, pl.ds(pl.multiple_of(16 * t, 16), 16)],
            rx.at[i, pl.ds(CAP * w, CAP)],
            y_ss.at[i, t],
            y_rs.at[i, w],
            w_peer(t),
        )

    def y_arrival(i, s):
        at = pl.ds(CAP * s, CAP)
        return remote(rx.at[i, at], rx.at[i, at], y_ss.at[i, s], y_rs.at[i, s], w_peer(s))

    def gather_piece(i):
        for way in range(2):
            ag_arrival(i, way, hops(i, way) - 1).wait_recv()

        def one(n, carry):
            pick = pa[pl.ds(3 * n, 3)].reshape(3 * LANES, Z * TOK)
            yb[i, pl.ds(3 * n, 3)] = dot(pick, ga[i].reshape(Z * TOK, PC)).astype(BF16).reshape(3, LANES, PC)
            return carry

        lax.fori_loop(0, 3, one, 0)
        for o in range(1, W):
            y_copy(i, (w + o) % W).start()
        rx[i, pl.ds(CAP * w, CAP)] = yb[i, :, pl.ds(pl.multiple_of(16 * w, 16), 16)]

    def unit_of(i, j):
        u = 2 * piece_of(i) + j
        return u // 3, u % 3

    def rs_copy(i, j):
        owner, at = unit_of(i, j)
        return remote(su.at[2 * i + j], rs.at[at, dp], rs_ss.at[2 * i + j], rs_rs.at[at, dp], {"dp": owner})

    def rs_arrival(at, s):
        return remote(su.at[0], rs.at[at, s], rs_ss.at[0], rs_rs.at[at, s], {"dp": s})

    def product_piece(i):
        for o in range(1, W):
            y_arrival(i, (w + o) % W).wait_recv()
        for m in range(CAP):
            xt[:, m * LANES : (m + 1) * LANES] = rx[i, 8 * m : 8 * m + 8].reshape(LANES, PC).T

        def one(n, carry):
            at = pl.ds(pl.multiple_of(n * 256, 256), 256)
            out = dot(xt[...], hm[:, at]).astype(BF16)
            su[2 * i, :, at] = out[:UNIT]
            su[2 * i + 1, :, at] = out[UNIT:]
            return carry

        lax.fori_loop(0, 4, one, 0)
        for j in range(2):
            owner, at = unit_of(i, j)

            @pl.when(owner != dp)
            def _():
                rs_copy(i, j).start()

            @pl.when(owner == dp)
            def _():
                rs[at, dp] = su[2 * i + j]

    attend_plane()
    for i in range(PIECES):
        forward(i, 1)
    attend_carry()
    for i in range(2):
        forward(i, 2)
    hidden_plane()
    for slot in range(PIECES + 2):
        if slot + 2 < PIECES:
            forward(slot + 2, 2)
        if slot < PIECES:
            forward(slot, 3)
        if 0 <= slot - 1 < PIECES:
            gather_piece(slot - 1)
        if slot == 1:
            attend_last()
        if slot == 2:
            hidden_wide()
        if 0 <= slot - 2 < PIECES:
            product_piece(slot - 2)

    for o in range(1, DP):
        for at in range(3):
            rs_arrival(at, (dp + o) % DP).wait_recv()
    for at in range(3):
        acc[at * UNIT : (at + 1) * UNIT] = (
            (rs[at, 0].astype(F32) + rs[at, 1].astype(F32)) + (rs[at, 2].astype(F32) + rs[at, 3].astype(F32))
        )

    def turn(n, carry):
        at = pl.ds(pl.multiple_of(n * LANES, LANES), LANES)
        dg_ref[at, :] = acc[:, at].T.astype(BF16)
        return carry

    lax.fori_loop(0, 8, turn, 0)

    for i in range(PIECES):
        for way in range(2):
            for step in range(hops(i, way)):
                ag_copy(i, way, step).wait_send()
        for o in range(1, W):
            y_copy(i, (w + o) % W).wait_send()
        for j in range(2):
            @pl.when(unit_of(i, j)[0] != dp)
            def _():
                rs_copy(i, j).wait_send()
    for o in range(1, Z):
        hz_copy((z + o) % Z).wait_send()
        hw_copy((w + o) % W).wait_send()
        a_copy((w + o) % W).wait_send()
        c_copy((w + o) % W).wait_send()
    for t in range(Z - 1):
        @pl.when(t < z)
        def _():
            b_copy(t).wait_send()


def on_device(saved_pre, layer_grad, router_weight, routes, queries, key_vectors, value_vectors, head_grad, log_gate):
    vmem = pl.BlockSpec(memory_space=pltpu.VMEM)
    dma = pltpu.SemaphoreType.DMA
    key_grad, value_grad, down_grad = pl.pallas_call(
        kernel,
        out_shape=(
            jax.ShapeDtypeStruct((TOK, 1024), BF16),
            jax.ShapeDtypeStruct((TOK, 1024), BF16),
            jax.ShapeDtypeStruct((1024, OWN), BF16),
        ),
        in_specs=[vmem] * 9,
        out_specs=(vmem, vmem, vmem),
        scratch_shapes=[
            pltpu.VMEM((PIECES, Z, TOK, PC), BF16),
            pltpu.VMEM((PAIRS, FF), BF16),
            pltpu.VMEM((CAP, LANES, FF + LANES), BF16),
            pltpu.VMEM((CAP, Z, 16, FF + LANES), BF16),
            pltpu.VMEM((CAP, LANES, Z * TOK), BF16),
            pltpu.VMEM((CAP, LANES, FF), BF16),
            pltpu.VMEM((W * CAP, 16, FF), BF16),
            pltpu.VMEM((W * CAP * 16, 2 * FF), BF16),
            pltpu.VMEM((PIECES, CAP, LANES, PC), BF16),
            pltpu.VMEM((PIECES, W * CAP, 16, PC), BF16),
            pltpu.VMEM((PC, W * CAP * 16), BF16),
            pltpu.VMEM((12, UNIT, 2 * FF), BF16),
            pltpu.VMEM((3, DP, UNIT, 2 * FF), BF16),
            pltpu.VMEM((OWN, 2 * FF), F32),
            pltpu.VMEM((TOK, 1024), F32),
            pltpu.VMEM((W, LANES, LANES), F32),
            pltpu.VMEM((W, LANES, LANES), F32),
            pltpu.VMEM((LANES, LANES), F32),
            pltpu.VMEM((Z, LANES, LANES), F32),
            pltpu.VMEM((W, LANES, LANES), F32),
            pltpu.VMEM((W, 64, LANES), F32),
            pltpu.VMEM((W, 64, LANES), F32),
            dma((PIECES, 2, 4)),
            dma((PIECES, 2, 4)),
            dma((Z,)),
            dma((Z,)),
            dma((W,)),
            dma((W,)),
            dma((PIECES, W)),
            dma((PIECES, W)),
            dma((12,)),
            dma((3, DP)),
            dma((W,)),
            dma((W,)),
            dma((Z,)),
            dma((Z,)),
            dma((W,)),
            dma((W,)),
        ],
        compiler_params=pltpu.CompilerParams(
            collective_id=0, has_side_effects=True, vmem_limit_bytes=60 * 1024 * 1024
        ),
        cost_estimate=pl.CostEstimate(flops=16_000_000_000, bytes_accessed=8_000_000, transcendentals=1_000_000),
    )(
        saved_pre,
        layer_grad,
        routes.reshape(1, PAIRS),
        router_weight.reshape(1, PAIRS).astype(F32),
        queries[0],
        key_vectors[0],
        value_vectors[0],
        head_grad[0],
        log_gate[0],
    )
    return key_grad[None], value_grad[None], down_grad.reshape(2, FF, OWN)


def solution(mesh):
    return jax.shard_map(
        on_device,
        mesh=mesh,
        in_specs=(
            P(("dp", "ctx"), None, None),
            P(("dp", "ctx"), None),
            P(("dp", "ctx"), None),
            P(("dp", "ctx"), None),
            P("dp", "ctx", None),
            P("dp", "ctx", None),
            P("dp", "ctx", None),
            P("dp", "ctx", None),
            P("dp", "ctx", None),
        ),
        out_specs=(P("dp", "ctx", None), P("dp", "ctx", None), P("ctx", None, "dp")),
        check_vma=False,
    )
```

time: 612 us -> 181 us (0.30); the launches traced: 605 us -> 181 us
  waiting for transfers between devices: 264 us -> 0 us
  Pallas kernels: 0 us -> 173 us
  other arithmetic: 128 us -> 0 us
  local copies, waits for them, and re-layouts: 103 us -> 6.8 us
  blocking collectives: 56.9 us -> 0 us
  starting transfers between devices: 20.6 us -> 0 us
  between operations: 15.8 us -> 0.66 us
  matrix products: 15 us -> 0 us
    all_to_all x2 -> x0, waiting for transfers between devices: 188 us -> none  [the longest x1 149 us: on_device(): lax.all_to_all(sent_grad, 'ctx', split_axis=0, concat_axis=0, tiled=True)]
    pallas_call x0 -> x1, Pallas kernels: none -> 173 us  [on_device(): pl.pallas_call(kernel, out_shape=(jax.ShapeDtypeStruct((TOK, 1024), BF16)...]
    select_n x68 -> x0, other arithmetic: 88.2 us -> none  [the longest x64 88.2 us: hop(): return jax.tree.map(lambda a, b: jnp.where(reached, a, b), new, before)]
    all_gather x1 -> x0, waiting for transfers between devices: 76.1 us -> none  [carried_in(): everything = jax.tree.map(lambda part: lax.all_gather(part, axis), array)]
    all_gather x1 -> x0, blocking collectives: 56.9 us -> none  [carried_in(): everything = jax.tree.map(lambda part: lax.all_gather(part, axis), array)]
    mul x68 -> x0, local copies, waits for them, and re-layouts: 46.9 us -> none  [the longest x64 45 us: join_later(): return (later[0] * earlier[0], later[0][:, :, None] * earlier[1] + later[1])]
    another operation x3 -> x0, other arithmetic: 23.5 us -> none  [the longest x1 23.3 us: head_backward(): cumulative = jnp.cumsum(log_gate[0].reshape(shape), axis=0)]
    all_to_all x2 -> x0, starting transfers between devices: 20.3 us -> none  [the longest x1 13.5 us: on_device(): lax.all_to_all(sent_pre, 'ctx', split_axis=0, concat_axis=0, tiled=True)]
  transfers between devices with their start and end apart: 4 -> 0, of which waited for: 3 -> 0; matrix products, arithmetic and copies ran while one was open for 13% -> 0% of each run, Pallas kernels for 0% -> 0%
where the time goes in v1:
time: 181 us
  Pallas kernels  173 us (96%)
  local copies, waits for them, and re-layouts  6.8 us (4%)
    pallas_call x1, Pallas kernels, on_device(): pl.pallas_call(kernel, out_shape=(jax.ShapeDtypeStruct((TOK, 1024), BF16)...  173 us
    unnamed x8, local copies, waits for them, and re-layouts  4.63 us

profile of v1, /device:TPU:1, one launch (start us, length us, event | category | flops | bytes accessed | tf_op | source)
XLA Modules:
  0.0 180.8 jit_solution(8469536606570948835)
XLA Ops:
  0.6 0.8 copy.16
  1.4 0.7 reshape.29.wt_ref
  2.1 0.8 copy.15
  2.9 0.7 reshape.27.rt_ref
  3.6 173.4 %shard_map.112 = (bf16[128,1024]{1,0:T(8,128)(2,1)}, bf16[128,1024]{1,0:T(8,128)(2,1)}, bf16[1024,576]{1,0:T(8,128)(2,1)}) custom-call(bf16[128,8,1024]{2,1,0:T(8,128)(2,1)} %pre_ref.1, bf16[128,2304]{1,0:T(8,128)(2,1)} %g_ref.1, s32[1,1024]{1,0:T(1,128)} %reshape.27.rt_ref, f32[1,1024]{1,0:T(1,128)} %reshape.29.wt_ref, bf16[128,1024]{1,0:T(8,128)(2,1)} %bitcast.12, ...), custom_call_target="tpu_custom_call" | custom-call | flops 16000000000 | bytes 8000000 | tf_op jit(solution)/shard_map/pallas_call | solution.py:434
  177.0 0.0 copy-start.1
  177.0 0.0 copy-start
  177.0 2.4 %copy.17 = bf16[2,512,576]{1,2,0:T(8,128)(2,1)} copy(bf16[2,512,576]{2,1,0:T(8,128)(2,1)} %bitcast.8) | data formatting | bytes 2359296
  179.4 0.0 copy-done.1
  179.4 0.7 copy.20
  180.1 0.0 copy-done
  180.1 0.7 copy.21
Async XLA Ops:
  177.0 2.5 %copy-start.1 = (bf16[128,1024]{1,0:T(8,128)(2,1)S(1)}, bf16[128,1024]{1,0:T(8,128)(2,1)}, u32[]{:S(2)}) copy-start(bf16[128,1024]{1,0:T(8,128)(2,1)} %get-tuple-element.6) | copy-start | bytes 786436
  177.0 3.1 %copy-start = (bf16[128,1024]{1,0:T(8,128)(2,1)S(1)}, bf16[128,1024]{1,0:T(8,128)(2,1)}, u32[]{:S(2)}) copy-start(bf16[128,1024]{1,0:T(8,128)(2,1)} %get-tuple-element.7) | copy-start | bytes 786436

commit v2 on v1

v2 whole, which is shorter than its diff:
```python
import functools

import jax
import jax.numpy as jnp
from jax import lax
from jax.experimental import pallas as pl
from jax.experimental.pallas import tpu as pltpu
from jax.sharding import PartitionSpec as P

FF = 512
HALF = FF // 2
TOK = 128
D = 2304
Z = 8
W = 8
DP = 4
CAP = 9
TOP = 8
PAIRS = TOK * TOP
PIECES = 6
PC = D // PIECES
UNIT = D // 12
OWN = D // DP
LANES = 128
MESH = pl.DeviceIdType.MESH
F32 = jnp.float32
BF16 = jnp.bfloat16


def iota(shape, dim):
    return lax.broadcasted_iota(jnp.int32, shape, dim)


def dot(a, b):
    return lax.dot_general(a, b, (((1,), (0,)), ((), ())), preferred_element_type=F32)


def dot_nt(a, b):
    return lax.dot_general(a, b, (((1,), (1,)), ((), ())), preferred_element_type=F32)


def dot_tn(a, b):
    return lax.dot_general(a, b, (((0,), (0,)), ((), ())), preferred_element_type=F32)


def split2(x):
    hi = x.astype(BF16)
    return hi, (x - hi.astype(F32)).astype(BF16)


def kernel(
    pre_ref, g_ref, rt_ref, wt_ref, q_ref, k_ref, v_ref, do_ref, lg_ref,
    kg_ref, vg_ref, dg_ref,
    ga, hid, sh, hin, pa, hy, hr, hm, yb, rx, xt, su, rs, acc,
    cum, tb_s, tb_r, pt, a_s, a_r, b_s, b_r, cl, c_s, c_r,
    ag_ss, ag_rs, t_ss, t_rs, hz_ss, hz_rs, hw_ss, hw_rs, y_ss, y_rs, rs_ss, rs_rs,
    a_ss, a_rs, b_ss, b_rs, c_ss, c_rs,
):
    dp = lax.axis_index("dp")
    ctx = lax.axis_index("ctx")
    z = ctx // W
    w = ctx % W

    def z_peer(t):
        return {"ctx": t * W + w}

    def w_peer(t):
        return {"ctx": z * W + t}

    def remote(src, dst, ss, rsem, dev):
        return pltpu.make_async_remote_copy(
            src_ref=src, dst_ref=dst, send_sem=ss, recv_sem=rsem, device_id=dev, device_id_type=MESH
        )

    barrier = pltpu.get_barrier_semaphore()
    for o in range(1, Z):
        pl.semaphore_signal(barrier, inc=1, device_id=z_peer((z + o) % Z), device_id_type=MESH)
        pl.semaphore_signal(barrier, inc=1, device_id=w_peer((w + o) % W), device_id_type=MESH)
    for o in range(1, DP):
        pl.semaphore_signal(barrier, inc=1, device_id={"dp": (dp + o) % DP}, device_id_type=MESH)

    def all_here():
        pl.semaphore_wait(barrier, (Z - 1) + (W - 1) + (DP - 1))

    first_piece = (2 + (3 * dp) // 2) % PIECES

    def piece_of(i):
        return (first_piece + i) % PIECES

    def hops(i, way):
        return 4 if (i % 2 == 0) == (way == 0) else 3

    def ag_copy(i, way, step):
        src = (z - step + Z) % Z if way == 0 else (z + step) % Z
        to = (z + 1) % Z if way == 0 else (z + Z - 1) % Z
        return remote(ga.at[i, src], ga.at[i, src], ag_ss.at[i, way, step], ag_rs.at[i, way, step], z_peer(to))

    def ag_arrival(i, way, step):
        src = (z - 1 - step + 2 * Z) % Z if way == 0 else (z + 1 + step) % Z
        return remote(
            ga.at[i, src], ga.at[i, src], ag_ss.at[i, way, step], ag_rs.at[i, way, step], z_peer((z + 1) % Z)
        )

    def start_piece(i):
        ga[i, z] = g_ref[:, pl.ds(pl.multiple_of(piece_of(i) * PC, LANES), PC)]
        ag_copy(i, 0, 0).start()
        ag_copy(i, 1, 0).start()

    def forward(i, step):
        for way in range(2):
            if step < hops(i, way):
                ag_arrival(i, way, step - 1).wait_recv()
                ag_copy(i, way, step).start()

    def t_copy(t):
        return remote(tb_s, tb_r.at[z], t_ss.at[t], t_rs.at[z], z_peer(t))

    def t_arrival(s):
        return remote(tb_s, tb_r.at[s], t_ss.at[s], t_rs.at[s], z_peer(s))

    def make_tables():
        tb_s[:TOP] = rt_ref[...].astype(F32)
        tb_s[TOP:] = wt_ref[...].astype(F32)

    def send_tables():
        for o in range(1, Z):
            t_copy((z + o) % Z).start()
        tb_r[z] = tb_s[...]

    before = jnp.where(iota((TOK, TOK), 0) < iota((TOK, TOK), 1), 1.0, 0.0).astype(BF16)

    def hidden_first():
        def hidden_block(n, carry):
            x = pre_ref[pl.ds(n * 16, 16)].astype(F32).reshape(LANES, 2 * FF)
            gate, up = x[:, :FF], x[:, FF:]
            hid[pl.ds(pl.multiple_of(n * LANES, LANES), LANES), :] = (gate / (1.0 + jnp.exp(-gate)) * up).astype(BF16)
            return carry

        lax.fori_loop(0, PAIRS // LANES, hidden_block, 0)

    def expert_at(shape):
        row = iota(shape, 0)
        return (row // 2) % 8 * 16 + row // 16 * 2 + row % 2

    def hidden_sort():
        expert = expert_at((LANES, TOK)).astype(F32)
        by_token = jnp.zeros((LANES, TOK), F32)
        for j in range(TOP):
            by_token = by_token + jnp.where(tb_s[j : j + 1] == expert, 1.0, 0.0)
        rank = dot(by_token.astype(BF16), before)
        rank = jnp.where(by_token > 0.5, rank, -1.0)
        token_of = jnp.where(iota((PAIRS, TOK), 0) // TOP == iota((PAIRS, TOK), 1), 1.0, 0.0).astype(BF16)
        wide = dot_nt(tb_s[:TOP].astype(BF16), token_of)
        chosen = iota((TOP, PAIRS), 0) == iota((TOP, PAIRS), 1) % TOP
        route = jnp.sum(jnp.where(chosen, wide, 0.0), axis=0, keepdims=True)
        rank_pair = jnp.where(route == expert_at((LANES, PAIRS)).astype(F32), dot_nt(rank.astype(BF16), token_of), -1.0)
        for r in range(CAP):
            pa[r] = jnp.where(rank_pair == float(r), 1.0, 0.0).astype(BF16)

        def sort_block(n, carry):
            pick = pa[pl.ds(3 * n, 3)].reshape(3 * LANES, PAIRS)
            x = dot(pick, hid[...]).astype(BF16)
            sh[0, pl.ds(3 * n, 3)] = x[:, :HALF].reshape(3, LANES, HALF)
            sh[1, pl.ds(3 * n, 3)] = x[:, HALF:].reshape(3, LANES, HALF)
            return carry

        lax.fori_loop(0, 3, sort_block, 0)

    def hw_copy(h, t):
        at = pl.ds(pl.multiple_of(16 * t, 16), 16)
        return remote(sh.at[h, :, at], hin.at[h, :, w], hw_ss.at[h, t], hw_rs.at[h, w], w_peer(t))

    def hw_arrival(h, s):
        return remote(hin.at[h, :, w], hin.at[h, :, s], hw_ss.at[h, s], hw_rs.at[h, s], w_peer(s))

    def hidden_send(h):
        for o in range(1, W):
            hw_copy(h, (w + o) % W).start()
        hin[h, :, w] = sh[h, :, pl.ds(pl.multiple_of(16 * w, 16), 16)]

    lane = iota((LANES, LANES), 1)
    low = lane < 64
    low64 = iota((64, LANES), 1) < 64
    tri = jnp.where(iota((TOK, TOK), 1) <= iota((TOK, TOK), 0), 1.0, 0.0).astype(BF16)

    def attend_first(j, carry):
        at = pl.ds(pl.multiple_of(j * LANES, LANES), LANES)
        x = lg_ref[:, at]
        hi, rest = split2(x)
        mid, lo = split2(x - hi.astype(F32))
        total = dot(tri, hi) + (dot(tri, mid) + dot(tri, lo))
        cum[:, at] = total
        qh, ql = split2(q_ref[:, at].astype(F32) * jnp.exp(total))
        do = do_ref[:, at]
        s = dot_tn(qh, do) + dot_tn(ql, do)
        a_s[j, :64] = jnp.where(low64, s[:64], s[64:])
        a_s[j, 64:] = jnp.broadcast_to(total[TOK - 1 :], (8, LANES))
        return carry

    def a_copy(t):
        return remote(a_s.at[t], a_r.at[w], a_ss.at[t], a_rs.at[w], w_peer(t))

    def a_arrival(s):
        return remote(a_s.at[s], a_r.at[s], a_ss.at[s], a_rs.at[s], w_peer(s))

    def attend_block():
        lax.fori_loop(0, W, attend_first, 0)

    def attend_send():
        for o in range(1, W):
            a_copy((w + o) % W).start()
        a_r[w] = a_s[w]

    def down_channels(row):
        x = jnp.broadcast_to(row, (LANES, LANES)).T
        return jnp.where(low64, x[:64], x[64:])

    def b_copy(t):
        return remote(b_s, b_r.at[z], b_ss.at[t], b_rs.at[z], z_peer(t))

    def b_arrival(s):
        return remote(b_s, b_r.at[s], b_ss.at[s], b_rs.at[s], z_peer(s))

    def attend_plane():
        for o in range(1, W):
            a_arrival((w + o) % W).wait_recv()
        c = jnp.zeros((64, LANES), F32)
        d = jnp.zeros((64, LANES), F32)
        whole = jnp.zeros((8, LANES), F32)
        for b in range(W - 1, -1, -1):
            cl[b, :64] = c
            cl[b, 64:] = d
            ld = down_channels(a_r[b, 64:65])
            c = a_r[b, :64] + jnp.exp(ld) * c
            d = d + ld
            whole = whole + a_r[b, 64:]
        b_s[:64] = c
        b_s[64:] = whole
        for t in range(Z - 1):
            @pl.when(t < z)
            def _():
                b_copy(t).start()

    def c_copy(t):
        return remote(c_s.at[t], c_r.at[w], c_ss.at[t], c_rs.at[w], w_peer(t))

    def c_arrival(s):
        return remote(c_s.at[s], c_r.at[s], c_ss.at[s], c_rs.at[s], w_peer(s))

    def attend_carry():
        acc[...] = jnp.zeros((64, LANES), F32)
        for s in range(Z - 1, 0, -1):
            @pl.when(s > z)
            def _():
                b_arrival(s).wait_recv()
                acc[...] = b_r[s, :64] + jnp.exp(down_channels(b_r[s, 64:65])) * acc[...]
        x = acc[...]
        for b in range(W):
            c_s[b] = cl[b, :64] + jnp.exp(cl[b, 64:]) * x
        for o in range(1, W):
            c_copy((w + o) % W).start()
        c_r[w] = c_s[w]

    def attend_last():
        for o in range(1, W):
            c_arrival((w + o) % W).wait_recv()
        later = iota((TOK, TOK), 0) <= iota((TOK, TOK), 1)

        def pair(j, carry):
            at = pl.ds(pl.multiple_of(j * LANES, LANES), LANES)
            total = cum[:, at]
            middle = total[63:64]
            ek = jnp.exp(middle - total)
            tail = jnp.exp(total[TOK - 1 :] - total)
            k = k_ref[:, at].astype(F32)
            v = v_ref[:, at]
            do = do_ref[:, at]
            qs = q_ref[:, at].astype(F32) * jnp.exp(total - middle)
            ks = k * ek
            qh, ql = split2(qs)
            vo = jnp.zeros((TOK, LANES), F32)
            ko = jnp.zeros((TOK, LANES), F32)
            for half in (low, jnp.logical_not(low)):
                kh, kl = split2(jnp.where(half, ks, 0.0))
                scores = dot_nt(kh, qh) + (dot_nt(kh, ql) + dot_nt(kl, qh))
                sh_, sl_ = split2(jnp.where(later, scores, 0.0))
                dom = jnp.where(half, do.astype(F32), 0.0).astype(BF16)
                vo = vo + (dot(sh_, dom) + dot(sl_, dom))
                vm = jnp.where(half, v.astype(F32), 0.0).astype(BF16)
                bh, bl = split2(jnp.where(later, dot_nt(vm, do), 0.0))
                qmh, qml = split2(jnp.where(half, qs, 0.0))
                ko = ko + (dot(bh, qmh) + (dot(bl, qmh) + dot(bh, qml)))
            c = c_r[j]
            ch, clo = split2(jnp.concatenate([jnp.where(low64, c, 0.0), jnp.where(low64, 0.0, c)], axis=0))
            th, tl = split2(k * tail)
            vo = vo + (dot(th, ch) + (dot(th, clo) + dot(tl, ch)))
            ko = ek * ko + tail * (dot_nt(v, ch) + dot_nt(v, clo))
            kg_ref[:, at] = ko.astype(BF16)
            vg_ref[:, at] = vo.astype(BF16)
            return carry

        lax.fori_loop(0, W, pair, 0)

    def hz_copy(h, t):
        at = pl.ds(pl.multiple_of(16 * t, 16), 16)
        return remote(hy.at[h, :, at], hr.at[h, :, z], hz_ss.at[h, t], hz_rs.at[h, z], z_peer(t))

    def hz_arrival(h, s):
        return remote(hr.at[h, :, z], hr.at[h, :, s], hz_ss.at[h, s], hz_rs.at[h, s], z_peer(s))

    def placing():
        row = iota((LANES, LANES), 0)
        col = iota((LANES, LANES), 1)
        same = (row // 2) % 8 == col // 16
        return jnp.where(same & (col % 16 == 2 * (row // 16) + row % 2), 1.0, 0.0).astype(BF16)

    def weights_plane():
        for o in range(1, Z):
            t_arrival((z + o) % Z).wait_recv()
        expert = (iota((16, TOK), 0) + 16 * z).astype(F32)
        for s in range(Z):
            count = jnp.zeros((16, TOK), F32)
            weight = jnp.zeros((16, TOK), F32)
            for j in range(TOP):
                hit = tb_r[s, j : j + 1] == expert
                count = count + jnp.where(hit, 1.0, 0.0)
                weight = weight + jnp.where(hit, tb_r[s, TOP + j : TOP + j + 1], 0.0)
            pt[16 * s : 16 * s + 16] = count
            pt[LANES + 16 * s : LANES + 16 * s + 16] = weight
        count = pt[:LANES]
        rank = jnp.where(count > 0.5, dot(count.astype(BF16), before), -1.0)
        rank = dot(placing(), rank.astype(BF16))
        weight = dot(placing(), pt[LANES:].astype(BF16))
        source = (iota((LANES, TOK), 0) // 2) % Z
        for r in range(CAP):
            mine = jnp.where(rank == float(r), weight, 0.0)
            for s in range(Z):
                pa[r, :, s * LANES : (s + 1) * LANES] = jnp.where(source == s, mine, 0.0).astype(BF16)

    def hidden_plane(h):
        for o in range(1, W):
            hw_arrival(h, (w + o) % W).wait_recv()

        def one(r, carry):
            hy[h, r] = dot(placing(), hin[h, r].reshape(LANES, HALF)).astype(BF16)
            return carry

        lax.fori_loop(0, CAP, one, 0)
        for o in (4, 3, 5, 2, 6, 1, 7):
            hz_copy(h, (z + o) % Z).start()
        hr[h, :, z] = hy[h, :, pl.ds(pl.multiple_of(16 * z, 16), 16)]

    def hidden_wide(h):
        for o in range(1, Z):
            hz_arrival(h, (z + o) % Z).wait_recv()

        def one(r, carry):
            x = dot(placing(), hr[h, r].reshape(LANES, HALF))
            first = iota((LANES, HALF), 0) % 2 == 0
            left = jnp.where(first, x, 0.0).astype(BF16)
            right = jnp.where(first, 0.0, x).astype(BF16)
            for s in range(W):
                at = pl.ds(pl.multiple_of(16 * (CAP * s + r), 16), 16)
                hm[h, at, :HALF] = left[16 * s : 16 * s + 16]
                hm[h, at, HALF:] = right[16 * s : 16 * s + 16]
            return carry

        lax.fori_loop(0, CAP, one, 0)

    def y_copy(i, t):
        return remote(
            yb.at[i, :, pl.ds(pl.multiple_of(16 * t, 16), 16)],
            rx.at[i, pl.ds(CAP * w, CAP)],
            y_ss.at[i, t],
            y_rs.at[i, w],
            w_peer(t),
        )

    def y_arrival(i, s):
        at = pl.ds(CAP * s, CAP)
        return remote(rx.at[i, at], rx.at[i, at], y_ss.at[i, s], y_rs.at[i, s], w_peer(s))

    def gather_piece(i):
        for way in range(2):
            ag_arrival(i, way, hops(i, way) - 1).wait_recv()

        def one(n, carry):
            pick = pa[pl.ds(3 * n, 3)].reshape(3 * LANES, Z * TOK)
            yb[i, pl.ds(3 * n, 3)] = dot(pick, ga[i].reshape(Z * TOK, PC)).astype(BF16).reshape(3, LANES, PC)
            return carry

        lax.fori_loop(0, 3, one, 0)
        for o in range(1, W):
            y_copy(i, (w + o) % W).start()
        rx[i, pl.ds(CAP * w, CAP)] = yb[i, :, pl.ds(pl.multiple_of(16 * w, 16), 16)]

    def unit_of(i, j):
        u = 2 * piece_of(i) + j
        return u // 3, u % 3

    def rs_copy(i, h, j):
        owner, at = unit_of(i, j)
        return remote(
            su.at[h, 2 * i + j], rs.at[h, at, dp], rs_ss.at[h, 2 * i + j], rs_rs.at[h, at, dp], {"dp": owner}
        )

    def rs_arrival(h, at, s):
        return remote(su.at[h, 0], rs.at[h, at, s], rs_ss.at[h, 0], rs_rs.at[h, at, s], {"dp": s})

    def rows_piece(i):
        for o in range(1, W):
            y_arrival(i, (w + o) % W).wait_recv()
        for m in range(CAP):
            xt[i, :, m * LANES : (m + 1) * LANES] = rx[i, 8 * m : 8 * m + 8].reshape(LANES, PC).T

    def product_piece(i, h):
        def one(n, carry):
            at = pl.ds(pl.multiple_of(n * 256, 256), 256)
            out = dot(xt[i], hm[h, :, at]).astype(BF16)
            su[h, 2 * i, :, at] = out[:UNIT]
            su[h, 2 * i + 1, :, at] = out[UNIT:]
            return carry

        lax.fori_loop(0, 2, one, 0)
        for j in range(2):
            owner, at = unit_of(i, j)

            @pl.when(owner != dp)
            def _():
                rs_copy(i, h, j).start()

            @pl.when(owner == dp)
            def _():
                rs[h, at, dp] = su[h, 2 * i + j]

    make_tables()
    hidden_first()
    hidden_sort()
    attend_block()
    all_here()
    send_tables()
    attend_send()
    hidden_send(0)
    hidden_send(1)
    start_piece(0)
    start_piece(1)
    start_piece(2)
    weights_plane()
    forward(0, 1)
    forward(1, 1)
    forward(2, 1)
    attend_plane()
    forward(0, 2)
    forward(1, 2)
    forward(2, 2)
    forward(0, 3)
    forward(1, 3)
    forward(2, 3)
    hidden_plane(0)
    attend_carry()
    gather_piece(0)
    hidden_plane(1)
    start_piece(3)
    gather_piece(1)
    gather_piece(2)
    attend_last()
    start_piece(4)
    forward(3, 1)
    hidden_wide(0)
    rows_piece(0)
    product_piece(0, 0)
    forward(3, 2)
    start_piece(5)
    forward(4, 1)
    rows_piece(1)
    product_piece(1, 0)
    forward(3, 3)
    forward(4, 2)
    forward(5, 1)
    hidden_wide(1)
    product_piece(0, 1)
    product_piece(1, 1)
    rows_piece(2)
    product_piece(2, 0)
    product_piece(2, 1)
    gather_piece(3)
    forward(4, 3)
    forward(5, 2)
    gather_piece(4)
    forward(5, 3)
    gather_piece(5)
    rows_piece(3)
    product_piece(3, 0)
    product_piece(3, 1)
    rows_piece(4)
    product_piece(4, 0)
    product_piece(4, 1)
    rows_piece(5)
    product_piece(5, 0)
    product_piece(5, 1)

    for h in range(2):
        for at in range(3):
            for o in range(1, DP):
                rs_arrival(h, at, (dp + o) % DP).wait_recv()
            for e in range(2):
                cols = slice(e * HALF, (e + 1) * HALF)
                total = (rs[h, at, 0, :, cols].astype(F32) + rs[h, at, 1, :, cols].astype(F32)) + (
                    rs[h, at, 2, :, cols].astype(F32) + rs[h, at, 3, :, cols].astype(F32)
                )
                dg_ref[e, at * UNIT : (at + 1) * UNIT, h * HALF : (h + 1) * HALF] = total.astype(BF16)

    for i in range(PIECES):
        for way in range(2):
            for step in range(hops(i, way)):
                ag_copy(i, way, step).wait_send()
        for o in range(1, W):
            y_copy(i, (w + o) % W).wait_send()
        for j in range(2):
            @pl.when(unit_of(i, j)[0] != dp)
            def _():
                for h in range(2):
                    rs_copy(i, h, j).wait_send()
    for o in range(1, Z):
        t_copy((z + o) % Z).wait_send()
        for h in range(2):
            hz_copy(h, (z + o) % Z).wait_send()
            hw_copy(h, (w + o) % W).wait_send()
        a_copy((w + o) % W).wait_send()
        c_copy((w + o) % W).wait_send()
    for t in range(Z - 1):
        @pl.when(t < z)
        def _():
            b_copy(t).wait_send()


def on_device(saved_pre, layer_grad, router_weight, routes, queries, key_vectors, value_vectors, head_grad, log_gate):
    vmem = pl.BlockSpec(memory_space=pltpu.VMEM)
    dma = pltpu.SemaphoreType.DMA
    key_grad, value_grad, down_grad = pl.pallas_call(
        kernel,
        out_shape=(
            jax.ShapeDtypeStruct((TOK, 1024), BF16),
            jax.ShapeDtypeStruct((TOK, 1024), BF16),
            jax.ShapeDtypeStruct((2, OWN, FF), BF16),
        ),
        in_specs=[vmem] * 9,
        out_specs=(vmem, vmem, vmem),
        scratch_shapes=[
            pltpu.VMEM((PIECES, Z, TOK, PC), BF16),
            pltpu.VMEM((PAIRS, FF), BF16),
            pltpu.VMEM((2, CAP, LANES, HALF), BF16),
            pltpu.VMEM((2, CAP, W, 16, HALF), BF16),
            pltpu.VMEM((CAP, LANES, Z * TOK), BF16),
            pltpu.VMEM((2, CAP, LANES, HALF), BF16),
            pltpu.VMEM((2, CAP, Z, 16, HALF), BF16),
            pltpu.VMEM((2, W * CAP * 16, FF), BF16),
            pltpu.VMEM((PIECES, CAP, LANES, PC), BF16),
            pltpu.VMEM((PIECES, W * CAP, 16, PC), BF16),
            pltpu.VMEM((PIECES, PC, W * CAP * 16), BF16),
            pltpu.VMEM((2, 12, UNIT, FF), BF16),
            pltpu.VMEM((2, 3, DP, UNIT, FF), BF16),
            pltpu.VMEM((64, LANES), F32),
            pltpu.VMEM((TOK, 1024), F32),
            pltpu.VMEM((2 * TOP, TOK), F32),
            pltpu.VMEM((Z, 2 * TOP, TOK), F32),
            pltpu.VMEM((2 * LANES, TOK), F32),
            pltpu.VMEM((W, 72, LANES), F32),
            pltpu.VMEM((W, 72, LANES), F32),
            pltpu.VMEM((72, LANES), F32),
            pltpu.VMEM((Z, 72, LANES), F32),
            pltpu.VMEM((W, LANES, LANES), F32),
            pltpu.VMEM((W, 64, LANES), F32),
            pltpu.VMEM((W, 64, LANES), F32),
            dma((PIECES, 2, 4)),
            dma((PIECES, 2, 4)),
            dma((Z,)),
            dma((Z,)),
            dma((2, Z)),
            dma((2, Z)),
            dma((2, W)),
            dma((2, W)),
            dma((PIECES, W)),
            dma((PIECES, W)),
            dma((2, 12)),
            dma((2, 3, DP)),
            dma((W,)),
            dma((W,)),
            dma((Z,)),
            dma((Z,)),
            dma((W,)),
            dma((W,)),
        ],
        compiler_params=pltpu.CompilerParams(
            collective_id=0, has_side_effects=True, vmem_limit_bytes=60 * 1024 * 1024
        ),
        cost_estimate=pl.CostEstimate(flops=16_000_000_000, bytes_accessed=8_000_000, transcendentals=1_000_000),
    )(
        saved_pre,
        layer_grad,
        routes.T,
        router_weight.T,
        queries[0],
        key_vectors[0],
        value_vectors[0],
        head_grad[0],
        log_gate[0],
    )
    return key_grad[None], value_grad[None], jnp.swapaxes(down_grad, 1, 2)


def solution(mesh):
    return jax.shard_map(
        on_device,
        mesh=mesh,
        in_specs=(
            P(("dp", "ctx"), None, None),
            P(("dp", "ctx"), None),
            P(("dp", "ctx"), None),
            P(("dp", "ctx"), None),
            P("dp", "ctx", None),
            P("dp", "ctx", None),
            P("dp", "ctx", None),
            P("dp", "ctx", None),
            P("dp", "ctx", None),
        ),
        out_specs=(P("dp", "ctx", None), P("dp", "ctx", None), P("ctx", None, "dp")),
        check_vma=False,
    )
```

time: 181 us -> 147 us (0.81)
  Pallas kernels: 173 us -> 140 us
    pallas_call x1, Pallas kernels: 173 us -> 140 us  [on_device(): pl.pallas_call(kernel, out_shape=(jax.ShapeDtypeStruct((TOK, 1024), BF16)...]
    unnamed x8 -> x3, local copies, waits for them, and re-layouts: 4.63 us -> 5.7 us
where the time goes in v2:
time: 147 us; the launch traced here: 146 us
  Pallas kernels  140 us (95%)
  local copies, waits for them, and re-layouts  5.7 us (4%)
    pallas_call x1, Pallas kernels, on_device(): pl.pallas_call(kernel, out_shape=(jax.ShapeDtypeStruct((TOK, 1024), BF16)...  140 us
    unnamed x3, local copies, waits for them, and re-layouts  5.7 us

profile of v2, /device:TPU:1, one launch (start us, length us, event | category | flops | bytes accessed | tf_op | source)
XLA Modules:
  0.0 146.4 jit_solution(17726645522551601180)
XLA Ops:
  0.6 140.0 %shard_map.112 = (bf16[128,1024]{1,0:T(8,128)(2,1)}, bf16[128,1024]{1,0:T(8,128)(2,1)}, bf16[2,576,512]{2,1,0:T(8,128)(2,1)}) custom-call(bf16[128,8,1024]{2,1,0:T(8,128)(2,1)} %pre_ref.1, bf16[128,2304]{1,0:T(8,128)(2,1)} %g_ref.1, s32[8,128]{1,0:T(8,128)} %bitcast.18, bf16[8,128]{1,0:T(8,128)(2,1)} %bitcast.19, bf16[128,1024]{1,0:T(8,128)(2,1)} %bitcast.14, ...), custom_call_target="tpu_custom_call" | custom-call | flops 16000000000 | bytes 8000000 | tf_op jit(solution)/shard_map/pallas_call | solution.py:540
  140.7 1.7 %copy.15 = bf16[1,128,1024]{2,1,0:T(8,128)(2,1)} copy(bf16[1,128,1024]{2,1,0:T(8,128)(2,1)} %bitcast.12) | data formatting | bytes 524288
  142.4 1.7 %copy.16 = bf16[1,128,1024]{2,1,0:T(8,128)(2,1)} copy(bf16[1,128,1024]{2,1,0:T(8,128)(2,1)} %bitcast.11) | data formatting | bytes 524288
  144.0 2.4 %copy.17 = bf16[2,512,576]{1,2,0:T(8,128)(2,1)} copy(bf16[2,512,576]{1,2,0:T(8,128)(2,1)} %bitcast.10) | data formatting | bytes 2359296

commit v3 on v2

--- a/solution.py
+++ b/solution.py
@@ -460,38 +460,38 @@
     attend_carry()
     gather_piece(0)
     hidden_plane(1)
+    gather_piece(1)
     start_piece(3)
-    gather_piece(1)
-    gather_piece(2)
     attend_last()
-    start_piece(4)
-    forward(3, 1)
     hidden_wide(0)
     rows_piece(0)
     product_piece(0, 0)
-    forward(3, 2)
-    start_piece(5)
-    forward(4, 1)
+    forward(3, 1)
+    start_piece(4)
+    gather_piece(2)
     rows_piece(1)
     product_piece(1, 0)
+    forward(3, 2)
+    forward(4, 1)
+    hidden_wide(1)
+    product_piece(0, 1)
+    product_piece(1, 1)
+    start_piece(5)
     forward(3, 3)
     forward(4, 2)
     forward(5, 1)
-    hidden_wide(1)
-    product_piece(0, 1)
-    product_piece(1, 1)
+    gather_piece(3)
     rows_piece(2)
     product_piece(2, 0)
     product_piece(2, 1)
-    gather_piece(3)
     forward(4, 3)
     forward(5, 2)
     gather_piece(4)
     forward(5, 3)
-    gather_piece(5)
     rows_piece(3)
     product_piece(3, 0)
     product_piece(3, 1)
+    gather_piece(5)
     rows_piece(4)
     product_piece(4, 0)
     product_piece(4, 1)

time: 147 us -> 145 us (0.986)
  Pallas kernels: 140 us -> 137 us
    pallas_call x1, Pallas kernels: 140 us -> 137 us  [on_device(): pl.pallas_call(kernel, out_shape=(jax.ShapeDtypeStruct((TOK, 1024), BF16)...]
where the time goes in v3:
time: 145 us; the launch traced here: 144 us
  Pallas kernels  137 us (94%)
  local copies, waits for them, and re-layouts  5.7 us (4%)
    pallas_call x1, Pallas kernels, on_device(): pl.pallas_call(kernel, out_shape=(jax.ShapeDtypeStruct((TOK, 1024), BF16)...  137 us
    unnamed x3, local copies, waits for them, and re-layouts  5.7 us

profile of v3, /device:TPU:1, one launch (start us, length us, event | category | flops | bytes accessed | tf_op | source)
XLA Modules:
  0.0 143.5 jit_solution(672121089617039757)
XLA Ops:
  0.6 137.2 %shard_map.112 = (bf16[128,1024]{1,0:T(8,128)(2,1)}, bf16[128,1024]{1,0:T(8,128)(2,1)}, bf16[2,576,512]{2,1,0:T(8,128)(2,1)}) custom-call(bf16[128,8,1024]{2,1,0:T(8,128)(2,1)} %pre_ref.1, bf16[128,2304]{1,0:T(8,128)(2,1)} %g_ref.1, s32[8,128]{1,0:T(8,128)} %bitcast.18, bf16[8,128]{1,0:T(8,128)(2,1)} %bitcast.19, bf16[128,1024]{1,0:T(8,128)(2,1)} %bitcast.14, ...), custom_call_target="tpu_custom_call" | custom-call | flops 16000000000 | bytes 8000000 | tf_op jit(solution)/shard_map/pallas_call | solution.py:540
  137.8 1.7 %copy.15 = bf16[1,128,1024]{2,1,0:T(8,128)(2,1)} copy(bf16[1,128,1024]{2,1,0:T(8,128)(2,1)} %bitcast.12) | data formatting | bytes 524288
  139.5 1.7 %copy.16 = bf16[1,128,1024]{2,1,0:T(8,128)(2,1)} copy(bf16[1,128,1024]{2,1,0:T(8,128)(2,1)} %bitcast.11) | data formatting | bytes 524288
  141.2 2.4 %copy.17 = bf16[2,512,576]{1,2,0:T(8,128)(2,1)} copy(bf16[2,512,576]{1,2,0:T(8,128)(2,1)} %bitcast.10) | data formatting | bytes 2359296
